TPU v7x, 32 devices: a whole 2x2x4 slice. The times are simulated.
32 devices in a mesh: dp: 16 (over z, x, core), fsdp: 2 (over y).
Axes of the slice: x: 2, y: 2, z: 4, core: 2. Of those that a mesh axis runs over, the one named last changes fastest.
Arguments:
- tokens: bfloat16 [12288, 8192], P(('dp', 'fsdp')), may hold values from -41 to 41
- norm_gain: bfloat16 [8192], replicated, may hold values from 0.099609375 to 1.8984375
- key_weight: bfloat16 [8192, 768], P('fsdp'), may hold values from -0.0625 to 0.0625
- key_cotangent: bfloat16 [12288, 768], P(('dp', 'fsdp')), may hold values from -0.125 to 0.125
- basis: bfloat16 [768, 512], replicated, may hold values from -0.21875 to 0.21875
- exp_avg: float32 [512, 8192], P('dp', 'fsdp'), may hold values from -4 to 4
- exp_avg_sq: float32 [512, 8192], P('dp', 'fsdp'), may hold values from 0.2 to 2
Outputs:
- keys: bfloat16 [12288, 768], P(('dp', 'fsdp'))
- new_exp_avg: float32 [512, 8192], P('dp', 'fsdp')
- new_exp_avg_sq: float32 [512, 8192], P('dp', 'fsdp')
- update: bfloat16 [8192, 768], P('fsdp')
All inputs are finite; a program needn't handle non-finite values.
Results may differ from a plain program's by a relative error of at most 0.0051.
Values may be sent and summed in bfloat16 or wider, within the bound.
A program may use at most 128 MiB of HBM per device.

v0:
```python
import jax
import jax.numpy as jnp
from jax import lax
from jax.sharding import PartitionSpec as P

STEP = 4


def outer_rows(left, right):
    return lax.dot_general(
        left, right, (((0,), (0,)), ((), ())), preferred_element_type=jnp.float32
    )


def per_device(tokens, norm_gain, key_weight, key_cotangent, basis, exp_avg, exp_avg_sq):
    values = tokens.astype(jnp.float32)
    scale = lax.rsqrt(jnp.mean(values * values, axis=-1, keepdims=True) + 1e-05)
    normed = (values * scale * norm_gain.astype(jnp.float32)).astype(jnp.bfloat16)
    keys = jnp.dot(
        normed,
        lax.all_gather(key_weight, "fsdp", axis=0, tiled=True),
        preferred_element_type=jnp.float32,
    ).astype(jnp.bfloat16)
    projected = jnp.dot(key_cotangent, basis, preferred_element_type=jnp.float32).astype(
        jnp.bfloat16
    )
    summed_rows = lax.psum_scatter(
        outer_rows(projected, normed), "dp", scatter_dimension=0, tiled=True
    )
    grad_t = lax.psum_scatter(summed_rows, "fsdp", scatter_dimension=1, tiled=True)
    new_exp_avg = 0.9 * exp_avg + 0.1 * grad_t
    new_exp_avg_sq = 0.95 * exp_avg_sq + 0.05 * grad_t * grad_t
    first = new_exp_avg / (1.0 - 0.9**STEP)
    second = new_exp_avg_sq / (1.0 - 0.95**STEP)
    normalized = (first / (jnp.sqrt(second) + 1e-08)).astype(jnp.bfloat16)
    whole_rank = lax.all_gather(normalized, "dp", axis=0, tiled=True)
    back = lax.dot_general(
        whole_rank, basis, (((0,), (1,)), ((), ())), preferred_element_type=jnp.float32
    )
    update = (0.25 * back).astype(jnp.bfloat16)
    return (keys, new_exp_avg, new_exp_avg_sq, update)


def solution(mesh):
    in_specs = (
        P(("dp", "fsdp"), None),
        P(),
        P("fsdp", None),
        P(("dp", "fsdp"), None),
        P(),
        P("dp", "fsdp"),
        P("dp", "fsdp"),
    )
    out_specs = (P(("dp", "fsdp"), None), P("dp", "fsdp"), P("dp", "fsdp"), P("fsdp", None))
    return jax.shard_map(
        per_device, mesh=mesh, in_specs=in_specs, out_specs=out_specs, check_vma=False
    )
```

profile of v0, /device:TPU:0, one launch (start us, length us, event | category | flops | bytes accessed | tf_op | source)
XLA Modules:
  0.0 448.8 jit_solution(3772171351306719697)
XLA Ops:
  7.2 0.0 copy-start
  7.2 0.0 reduce-scatter.3.cloned.1.call-start
  7.2 4.2 fusion
  11.4 0.7 convert_element_type.22
  12.1 0.0 copy-done
  12.1 11.0 %fusion.3 = f32[512,8192]{1,0:T(8,128)} fusion(bf16[384,8192]{1,0:T(8,128)(2,1)} %param.7, f32[8192]{0:T(1024)S(1)} %convert_element_type.22, f32[384]{0:T(512)S(1)} %add_rsqrt_fusion, bf16[384,768]{1,0:T(8,128)(2,1)} %param.10, bf16[768,512]{1,0:T(8,128)(2,1)S(1)} %copy-done), kind=kOutput, calls=%fused_computation.6 | convolution fusion | flops 3535994880 | bytes 24479232 | tf_op jit(solution)/shard_map/dot_general | solution.py:10
  23.1 0.0 copy-start.1
  23.1 0.0 copy-start.2
  23.1 0.0 reduce-scatter.3.cloned.1.call-update
  23.1 0.0 reduce-scatter.5.cloned.1.call-start
  23.2 181.4 %reduce-scatter.3.cloned.1.call-done = f32[32,8192]{1,0:T(8,128)} async-done(((f32[512,8192]{1,0:T(8,128)}), f32[32,8192]{1,0:T(8,128)}) %reduce-scatter.3.cloned.1.call-update) | async-done | bytes 1048592 | tf_op jit(solution)/shard_map/reduce_scatter | solution.py:27
  204.6 0.0 reduce-scatter.5.cloned.1.call-update
  204.6 0.0 all-gather.3.cloned.1.call-start
  204.6 0.7 all-gather.3.cloned.1.call-update
  205.3 0.0 all-gather.5.cloned.1.call-start
  205.4 20.8 %reduce-scatter.5.cloned.1.call-done = f32[32,4096]{1,0:T(8,128)} async-done(((f32[32,8192]{1,0:T(8,128)}), f32[32,4096]{1,0:T(8,128)}) %reduce-scatter.5.cloned.1.call-update) | async-done | bytes 524304 | tf_op jit(solution)/shard_map/reduce_scatter | solution.py:30
  226.1 0.0 copy-done.1
  226.2 0.0 copy-done.2
  226.2 2.3 divide_convert_fusion
  228.5 0.0 all-gather.5.cloned.1.call-update
  228.5 151.8 %all-gather.3.cloned.1.call-done = bf16[8192,768]{1,0:T(8,128)(2,1)} async-done(((bf16[4096,768]{1,0:T(8,128)(2,1)}), bf16[8192,768]{1,0:T(8,128)(2,1)}) %all-gather.3.cloned.1.call-update) | async-done | bytes 12582928 | tf_op jit(solution)/shard_map/all_gather | solution.py:21
  380.3 11.6 %fusion.7 = bf16[384,768]{1,0:T(8,128)(2,1)} fusion(bf16[8192,768]{1,0:T(8,128)(2,1)} %all-gather.3.cloned.1.call-done, bf16[384,8192]{1,0:T(8,128)(2,1)} %param.7, f32[8192]{0:T(1024)S(1)} %convert_element_type.22, f32[384]{0:T(512)S(1)} %add_rsqrt_fusion), kind=kOutput, calls=%fused_computation.8 | convolution fusion | flops 4844716032 | bytes 19498496 | tf_op jit(solution)/shard_map/dot_general | solution.py:19
  392.0 42.0 %all-gather.5.cloned.1.call-done = bf16[512,4096]{1,0:T(8,128)(2,1)} async-done(((bf16[32,4096]{1,0:T(8,128)(2,1)}), bf16[512,4096]{1,0:T(8,128)(2,1)}) %all-gather.5.cloned.1.call-update) | async-done | bytes 4194320 | tf_op jit(solution)/shard_map/all_gather | solution.py:36
  433.9 8.4 %multiply_convert_fusion = bf16[4096,768]{1,0:T(8,128)(2,1)} fusion(bf16[512,4096]{1,0:T(8,128)(2,1)} %all-gather.5.cloned.1.call-done, bf16[768,512]{1,0:T(8,128)(2,1)S(1)} %copy-done), kind=kOutput, calls=%fused_computation.5 | convolution fusion | flops 3227516928 | bytes 11272192 | tf_op jit(solution)/shard_map/dot_general | solution.py:37
  (1 shorter events, 0.0 us)
Async XLA Ops:
  7.2 5.0 %copy-start = (bf16[768,512]{1,0:T(8,128)(2,1)S(1)}, bf16[768,512]{1,0:T(8,128)(2,1)}, u32[]{:S(2)}) copy-start(bf16[768,512]{1,0:T(8,128)(2,1)} %param.11) | copy-start | bytes 2359300
  7.2 197.4 %reduce-scatter.3.cloned.1.call-start = ((), (), s32[]{:S(2)}) async-start(), calls=%async_computation.3 | async-start | bytes 17825792 | tf_op jit(solution)/shard_map/reduce_scatter | solution.py:27
  23.1 203.0 %copy-start.1 = (f32[32,4096]{1,0:T(8,128)S(1)}, f32[32,4096]{1,0:T(8,128)}, u32[]{:S(2)}) copy-start(f32[32,4096]{1,0:T(8,128)} %param.13) | copy-start | bytes 1572868
  23.1 203.0 %copy-start.2 = (f32[32,4096]{1,0:T(8,128)S(1)}, f32[32,4096]{1,0:T(8,128)}, u32[]{:S(2)}) copy-start(f32[32,4096]{1,0:T(8,128)} %param.12) | copy-start | bytes 1572868
  23.1 203.0 %reduce-scatter.5.cloned.1.call-start = ((), (), s32[]{:S(2)}) async-start(), calls=%async_computation.4 | async-start | bytes 1572864 | tf_op jit(solution)/shard_map/reduce_scatter | solution.py:30
  204.6 175.8 %all-gather.3.cloned.1.call-start = ((), (), s32[]{:S(2)}) async-start(), calls=%async_computation.2 | async-start | bytes 18874368 | tf_op jit(solution)/shard_map/all_gather | solution.py:21
  205.3 228.6 %all-gather.5.cloned.1.call-start = ((), (), s32[]{:S(2)}) async-start(), calls=%async_computation.5 | async-start | bytes 4456448 | tf_op jit(solution)/shard_map/all_gather | solution.py:36
Sparse Core Ops, SparseCore 0:
  23.3 181.2 reduce-scatter.2
  206.8 19.3 reduce-scatter.4
  227.8 152.5 all-gather.2
  383.2 50.7 all-gather.4
where the time goes:
time: 449 us
  waiting for transfers between devices  397 us (88%)
  matrix products  31 us (7%)
  between operations  13.8 us (3%)
  other arithmetic  7.22 us (2%)
    reduce_scatter x1, waiting for transfers between devices, per_device(): lax.psum_scatter(outer_rows(projected, normed), 'dp', scatter_dimension=0...  181 us
    all_gather x1, waiting for transfers between devices, per_device(): lax.all_gather(key_weight, 'fsdp', axis=0, tiled=True)  152 us
    all_gather x1, waiting for transfers between devices, per_device(): whole_rank = lax.all_gather(normalized, 'dp', axis=0, tiled=True)  42 us
    reduce_scatter x1, waiting for transfers between devices, per_device(): lax.psum_scatter(summed_rows, 'fsdp', scatter_dimension=1, tiled=True)  20.8 us
    dot_general x1, matrix products, per_device(): jnp.dot(normed, lax.all_gather(key_weight, 'fsdp', axis=0, tiled=True), p...  11.6 us
    dot_general x1, matrix products, outer_rows(): lax.dot_general(left, right, (((0,), (0,)), ((), ())), preferred_element_...  11 us
  transfers between devices with their start and end apart: 4, of which 4 were waited for; matrix products, arithmetic and copies ran while one was open for 3% of the time, Pallas kernels for 0%

commit v1 on v0

v1 whole, which is shorter than its diff:
```python
import functools

import jax
import jax.numpy as jnp
from jax import lax
from jax.experimental import pallas as pl
from jax.experimental.pallas import tpu as pltpu
from jax.sharding import PartitionSpec as P

STEP = 4
CHUNKS = 8
PIECES = 2
ROW_TILE = 16
MESH_ID = pl.DeviceIdType.MESH
BF16 = jnp.bfloat16
F32 = jnp.float32


def remote(src, dst, send_sem, recv_sem, to):
    return pltpu.make_async_remote_copy(
        src_ref=src, dst_ref=dst, send_sem=send_sem, recv_sem=recv_sem,
        device_id=to, device_id_type=MESH_ID,
    )


def kernel(
    n_dp, n_f,
    tok_hbm, gain_ref, w_hbm, cot_ref, basis_ref, m_ref, v_ref,
    keys_ref, m_out, v_out, whole_out,
    normed, w_all, proj, core_tx, core_rx, x_tx, x_rx, y_tx, y_rx, z_own, z_tx, z_rx,
    whole, acc,
    load_sem, core_s, core_r, x_s, x_r, y_s, y_r, z_s, z_r,
    gz_s, gz_r, gx_s, gx_r, gc_s, gc_r, w1_s, w1_r, w2_s, w2_r, w3_s, w3_r, out_sem,
):
    n_z = n_dp // 4
    dp = lax.axis_index("dp")
    y = lax.axis_index("fsdp")
    core = lax.rem(dp, 2)
    x = lax.rem(lax.div(dp, 2), 2)
    z = lax.div(dp, 4)
    other_core, other_x = 1 - core, 1 - x
    dev_core = (dp + 1 - 2 * core, y)
    dev_x = (dp + 2 - 4 * x, y)
    z_bit = lax.rem(z, 2)
    dev_pair = (dp + 4 - 8 * z_bit, y)

    def at_y(k):
        return lax.rem(y + k, n_f)

    def at_z(k):
        return lax.rem(z + k, n_z)

    def dev_z(zi):
        return (zi * 4 + x * 2 + core, y)

    d_f = w_hbm.shape[0]
    rows, d = normed.shape
    cw = d_f // CHUNKS
    r = proj.shape[3]
    quarter = d_f // 4
    piece = quarter // PIECES

    load_tok = pltpu.make_async_copy(tok_hbm, normed, load_sem.at[0])
    load_tok.start()

    barrier = pltpu.get_barrier_semaphore()
    peers = [dev_core, dev_x]
    peers += [(dp, at_y(k)) for k in range(1, n_f)]
    peers += [dev_z(at_z(k)) for k in range(1, n_z)]
    for peer in peers:
        pl.semaphore_signal(barrier, inc=1, device_id=peer, device_id_type=MESH_ID)
    pl.semaphore_wait(barrier, len(peers))

    my_q = core + 2 * z_bit
    pair_q = core + 2 * (1 - z_bit)

    def w_rows(q, p):
        return pl.ds(pl.multiple_of(q * quarter + p * piece, piece), piece)

    def w1(p, k):
        return remote(
            w_hbm.at[w_rows(my_q, p)], w_all.at[y, w_rows(my_q, p)],
            w1_s.at[p, k - 1], w1_r.at[p, k - 1], (dp, at_y(n_f - k)),
        )

    def w2(p, k, j):
        blk = w_all.at[at_y(k), w_rows(my_q, p)]
        return remote(blk, blk, w2_s.at[p, k - 1, j], w2_r.at[p, k - 1, j],
                      dev_pair if j == 0 else dev_core)

    def w3(p, k):
        blk = w_all.at[at_y(k), w_rows(pair_q, p)]
        return remote(blk, blk, w3_s.at[p, k - 1], w3_r.at[p, k - 1], dev_core)

    for p in range(PIECES):
        for k in range(1, n_f):
            w1(p, k).start()

    load_w = pltpu.make_async_copy(w_hbm, w_all.at[y], load_sem.at[1])
    load_w.start()

    projected = lax.dot_general(
        basis_ref[...], cot_ref[...], (((0,), (1,)), ((), ())), preferred_element_type=F32
    ).astype(BF16)
    proj[...] = projected.reshape(proj.shape)

    load_tok.wait()

    gain = gain_ref[...].astype(F32)

    @pl.loop(0, rows // ROW_TILE)
    def _(i):
        sl = pl.ds(pl.multiple_of(i * ROW_TILE, ROW_TILE), ROW_TILE)
        values = normed[sl, :].astype(F32)
        scale = lax.rsqrt(jnp.mean(values * values, axis=-1, keepdims=True) + 1e-05)
        normed[sl, :] = (values * scale * gain).astype(BF16)

    def cols(f, t):
        return pl.ds(pl.multiple_of(f * d_f + t * cw, cw), cw)

    def part(lhs, f, t):
        return jnp.dot(lhs, normed[:, cols(f, t)], preferred_element_type=F32)

    def core_copy(t):
        return remote(core_tx.at[t], core_rx.at[t], core_s.at[t], core_r.at[t], dev_core)

    def x_copy(t):
        return remote(x_tx.at[t], x_rx.at[t], x_s.at[t], x_r.at[t], dev_x)

    def y_copy(t, k):
        return remote(y_tx.at[t, k - 1], y_rx.at[t, k - 1], y_s.at[t, k - 1],
                      y_r.at[t, k - 1], (dp, at_y(k)))

    def z_copy(t, k):
        return remote(z_tx.at[t, at_z(k)], z_rx.at[t, k - 1], z_s.at[t, k - 1],
                      z_r.at[t, k - 1], dev_z(at_z(k)))

    def gz_send(t, k):
        blk = whole.at[t, z, x, core]
        return remote(blk, blk, gz_s.at[t, k - 1], gz_r.at[t, k - 1], dev_z(at_z(k)))

    def gx_send(t):
        blk = whole.at[t, :, x, core]
        return remote(blk, blk, gx_s.at[t], gx_r.at[t], dev_x)

    def gc_send(t):
        blk = whole.at[t, :, :, core]
        return remote(blk, blk, gc_s.at[t], gc_r.at[t], dev_core)

    def stage_core(t):
        lhs = proj[:, :, other_core].reshape(n_z * 2 * r, rows)
        for f in range(n_f):
            core_tx[t, f] = part(lhs, f, t).astype(BF16).reshape(core_tx.shape[2:])
        core_copy(t).start()

    def stage_x(t):
        core_copy(t).wait_recv()
        lhs = proj[:, other_x, core].reshape(n_z * r, rows)
        for f in range(n_f):
            mine = part(lhs, f, t).reshape(n_z, r, cw)
            x_tx[t, f] = (mine + core_rx[t, f, :, other_x].astype(F32)).astype(BF16)
        x_copy(t).start()

    def chip_sum(f, t):
        mine = part(proj[:, x, core].reshape(n_z * r, rows), f, t).reshape(n_z, r, cw)
        return mine + core_rx[t, f, :, x].astype(F32) + x_rx[t, f].astype(F32)

    def stage_y(t):
        x_copy(t).wait_recv()
        for k in range(1, n_f):
            y_tx[t, k - 1] = chip_sum(at_y(k), t).astype(BF16)
            y_copy(t, k).start()

    def stage_z(t):
        for k in range(1, n_f):
            y_copy(t, k).wait_recv()
        total = chip_sum(y, t)
        for k in range(1, n_f):
            total = total + y_rx[t, k - 1].astype(F32)
        z_own[t] = total
        z_tx[t] = total.astype(BF16)
        for k in range(1, n_z):
            z_copy(t, k).start()

    def stage_adam(t):
        for k in range(1, n_z):
            z_copy(t, k).wait_recv()
        grad = z_own[t, z]
        for k in range(1, n_z):
            grad = grad + z_rx[t, k - 1].astype(F32)
        sl = pl.ds(pl.multiple_of(t * cw, cw), cw)
        m = 0.9 * m_ref[:, sl] + 0.1 * grad
        v = 0.95 * v_ref[:, sl] + 0.05 * grad * grad
        m_out[:, sl] = m
        v_out[:, sl] = v
        first = m / (1.0 - 0.9**STEP)
        second = v / (1.0 - 0.95**STEP)
        whole[t, z, x, core] = (first / (jnp.sqrt(second) + 1e-08)).astype(BF16)
        for k in range(1, n_z):
            gz_send(t, k).start()

    def stage_gx(t):
        for k in range(1, n_z):
            gz_send(t, k).wait_recv()
        gx_send(t).start()

    def stage_gc(t):
        gx_send(t).wait_recv()
        gc_send(t).start()

    def keys_part(f, t):
        rhs = w_all[f, pl.ds(pl.multiple_of(t * cw, cw), cw), :]
        return jnp.dot(normed[:, cols(f, t)], rhs, preferred_element_type=F32)

    def w_forward(p):
        for k in range(1, n_f):
            w1(p, k).wait_recv()
            w2(p, k, 0).start()
            w2(p, k, 1).start()

    def w_last(p):
        for k in range(1, n_f):
            w2(p, k, 0).wait_recv()
            w3(p, k).start()

    load_w.wait()
    acc[...] = jnp.zeros_like(acc)
    stages = [stage_core, stage_x, stage_y, stage_z, stage_adam, stage_gx, stage_gc]
    w_steps = {4: [(w_forward, 0)], 6: [(w_forward, 1)], 9: [(w_last, 0)], 12: [(w_last, 1)]}

    @pl.loop(0, CHUNKS + len(stages) - 1)
    def _(s):
        for lag, stage in reversed(list(enumerate(stages))):
            @pl.when(jnp.logical_and(s >= lag, s < CHUNKS + lag))
            def _():
                stage(s - lag)

        @pl.when(s < CHUNKS)
        def _():
            acc[...] += keys_part(y, s)

        for at, calls in w_steps.items():
            @pl.when(s == at)
            def _():
                for call, p in calls:
                    call(p)

    for p in range(PIECES):
        for k in range(1, n_f):
            w2(p, k, 1).wait_recv()
            w3(p, k).wait_recv()

    for k in range(1, n_f):
        @pl.loop(0, CHUNKS)
        def _(t):
            acc[...] += keys_part(at_y(k), t)

    keys_ref[...] = acc[...].astype(BF16)

    def out_copy(t):
        return pltpu.make_async_copy(whole.at[t], whole_out.at[t], out_sem.at[t])

    @pl.loop(0, CHUNKS)
    def _(t):
        gc_send(t).wait_recv()
        out_copy(t).start()

    @pl.loop(0, CHUNKS)
    def _(t):
        core_copy(t).wait_send()
        x_copy(t).wait_send()
        for k in range(1, n_f):
            y_copy(t, k).wait_send()
        for k in range(1, n_z):
            z_copy(t, k).wait_send()
            gz_send(t, k).wait_send()
        gx_send(t).wait_send()
        gc_send(t).wait_send()
        out_copy(t).wait()

    for p in range(PIECES):
        for k in range(1, n_f):
            w1(p, k).wait_send()
            w2(p, k, 0).wait_send()
            w2(p, k, 1).wait_send()
            w3(p, k).wait_send()


def per_device(n_dp, n_f, tokens, norm_gain, key_weight, key_cotangent, basis, exp_avg, exp_avg_sq):
    rows, d = tokens.shape
    d_f, kv = key_weight.shape
    rank = basis.shape[1]
    r = exp_avg.shape[0]
    n_z = n_dp // 4
    cw = d_f // CHUNKS
    c = CHUNKS
    vm = pl.BlockSpec(memory_space=pltpu.VMEM)
    hbm = pl.BlockSpec(memory_space=pl.ANY)
    dma = pltpu.SemaphoreType.DMA
    keys, m_new, v_new, whole = pl.pallas_call(
        functools.partial(kernel, n_dp, n_f),
        out_shape=(
            jax.ShapeDtypeStruct((rows, kv), BF16),
            jax.ShapeDtypeStruct(exp_avg.shape, F32),
            jax.ShapeDtypeStruct(exp_avg.shape, F32),
            jax.ShapeDtypeStruct((c, n_z, 2, 2, r, cw), BF16),
        ),
        in_specs=[hbm, vm, hbm, vm, vm, vm, vm],
        out_specs=(vm, vm, vm, hbm),
        scratch_shapes=[
            pltpu.VMEM((rows, d), BF16),
            pltpu.VMEM((n_f, d_f, kv), BF16),
            pltpu.VMEM((n_z, 2, 2, r, rows), BF16),
            pltpu.VMEM((c, n_f, n_z, 2, r, cw), BF16),
            pltpu.VMEM((c, n_f, n_z, 2, r, cw), BF16),
            pltpu.VMEM((c, n_f, n_z, r, cw), BF16),
            pltpu.VMEM((c, n_f, n_z, r, cw), BF16),
            pltpu.VMEM((c, n_f - 1, n_z, r, cw), BF16),
            pltpu.VMEM((c, n_f - 1, n_z, r, cw), BF16),
            pltpu.VMEM((c, n_z, r, cw), F32),
            pltpu.VMEM((c, n_z, r, cw), BF16),
            pltpu.VMEM((c, n_z - 1, r, cw), BF16),
            pltpu.VMEM((c, n_z, 2, 2, r, cw), BF16),
            pltpu.VMEM((rows, kv), F32),
            dma((2,)),
            dma((c,)), dma((c,)),
            dma((c,)), dma((c,)),
            dma((c, n_f - 1)), dma((c, n_f - 1)),
            dma((c, n_z - 1)), dma((c, n_z - 1)),
            dma((c, n_z - 1)), dma((c, n_z - 1)),
            dma((c,)), dma((c,)),
            dma((c,)), dma((c,)),
            dma((PIECES, n_f - 1)), dma((PIECES, n_f - 1)),
            dma((PIECES, n_f - 1, 2)), dma((PIECES, n_f - 1, 2)),
            dma((PIECES, n_f - 1)), dma((PIECES, n_f - 1)),
            dma((c,)),
        ],
        compiler_params=pltpu.CompilerParams(
            collective_id=0, has_side_effects=True, vmem_limit_bytes=60 * 2**20
        ),
    )(tokens, norm_gain.reshape(1, d), key_weight, key_cotangent, basis, exp_avg, exp_avg_sq)
    back = lax.dot_general(
        whole.reshape(c, rank, cw), basis, (((1,), (1,)), ((), ())), preferred_element_type=F32
    )
    update = (0.25 * back).astype(BF16).reshape(d_f, kv)
    return keys, m_new, v_new, update


def solution(mesh):
    in_specs = (
        P(("dp", "fsdp"), None),
        P(),
        P("fsdp", None),
        P(("dp", "fsdp"), None),
        P(),
        P("dp", "fsdp"),
        P("dp", "fsdp"),
    )
    out_specs = (P(("dp", "fsdp"), None), P("dp", "fsdp"), P("dp", "fsdp"), P("fsdp", None))
    return jax.shard_map(
        functools.partial(per_device, mesh.shape["dp"], mesh.shape["fsdp"]),
        mesh=mesh, in_specs=in_specs, out_specs=out_specs, check_vma=False,
    )
```

time: 449 us -> 153 us (0.34)
  waiting for transfers between devices: 397 us -> 0 us
  Pallas kernels: 0 us -> 139 us
  matrix products: 31 us -> 8.51 us
  between operations: 13.8 us -> 0.67 us
  other arithmetic: 7.22 us -> 0 us
    reduce_scatter x2 -> x0, waiting for transfers between devices: 202 us -> none  [the longest x1 181 us: per_device(): lax.psum_scatter(outer_rows(projected, normed), 'dp', scatter_dimension=0...]
    all_gather x2 -> x0, waiting for transfers between devices: 194 us -> none  [the longest x1 152 us: per_device(): lax.all_gather(key_weight, 'fsdp', axis=0, tiled=True)]
    pallas_call x0 -> x1, Pallas kernels: none -> 139 us  [per_device(): pl.pallas_call(functools.partial(kernel, n_dp, n_f), out_shape=(jax.Shape...]
    dot_general x3 -> x1, matrix products: 31 us -> 8.51 us  [per_device(): lax.dot_general(whole.reshape(c, rank, cw), basis, (((1,), (1,)), ((), ()...]
  transfers between devices with their start and end apart: 4 -> 0, of which waited for: 4 -> 0; matrix products, arithmetic and copies ran while one was open for 3% -> 0% of each run, Pallas kernels for 0% -> 0%
where the time goes in v1:
time: 153 us; the launch traced here: 152 us
  Pallas kernels  139 us (91%)
  matrix products  8.51 us (6%)
  local copies, waits for them, and re-layouts  3.77 us (2%)
    pallas_call x1, Pallas kernels, per_device(): pl.pallas_call(functools.partial(kernel, n_dp, n_f), out_shape=(jax.Shape...  139 us
    dot_general x1, matrix products, per_device(): lax.dot_general(whole.reshape(c, rank, cw), basis, (((1,), (1,)), ((), ()...  8.51 us

profile of v1, /device:TPU:0, one launch (start us, length us, event | category | flops | bytes accessed | tf_op | source)
XLA Modules:
  0.0 152.4 jit_solution(12084281474390635920)
XLA Ops:
  0.6 1.4 reshape.17.gain_ref
  2.0 0.0 copy-start
  2.0 139.4 %shard_map.102 = (bf16[384,768]{1,0:T(8,128)(2,1)}, f32[32,4096]{1,0:T(8,128)}, f32[32,4096]{1,0:T(8,128)}, bf16[8,4,2,2,32,512]{5,4,3,2,1,0:T(8,128)(2,1)}) custom-call(bf16[384,8192]{1,0:T(8,128)(2,1)} %tok_hbm.1, bf16[1,8192]{1,0:T(2,128)(2,1)} %reshape.17.gain_ref, bf16[4096,768]{1,0:T(8,128)(2,1)} %w_hbm.1, bf16[384,768]{1,0:T(8,128)(2,1)} %cot_ref.1, ...), custom_call_target="tpu_custom_call" | custom-call | tf_op jit(solution)/shard_map/pallas_call | solution.py:300
  141.4 0.0 copy-done
  141.4 0.0 copy-start.1
  141.5 0.0 copy-start.3
  141.5 0.0 copy-start.2
  141.5 8.5 %multiply_convert_fusion = bf16[8,512,768]{2,1,0:T(8,128)(2,1)} fusion(bf16[8,512,512]{2,1,0:T(8,128)(2,1)} %bitcast.6, bf16[768,512]{1,0:T(8,128)(2,1)S(1)} %copy-done), kind=kOutput, calls=%fused_computation | convolution fusion | flops 3227516928 | bytes 11272192 | tf_op jit(solution)/shard_map/dot_general | solution.py:342
  150.0 0.0 copy-done.1
  150.0 0.8 copy.16
  150.8 0.0 copy-done.3
  150.8 0.8 copy.17
  151.6 0.0 copy-done.2
  151.6 0.8 copy.18
Async XLA Ops:
  2.0 139.5 %copy-start = (bf16[768,512]{1,0:T(8,128)(2,1)S(1)}, bf16[768,512]{1,0:T(8,128)(2,1)}, u32[]{:S(2)}) copy-start(bf16[768,512]{1,0:T(8,128)(2,1)} %basis_ref.1) | copy-start | bytes 2359300
  141.4 8.5 %copy-start.1 = (bf16[384,768]{1,0:T(8,128)(2,1)S(1)}, bf16[384,768]{1,0:T(8,128)(2,1)}, u32[]{:S(2)}) copy-start(bf16[384,768]{1,0:T(8,128)(2,1)} %get-tuple-element.16) | copy-start | bytes 1769476
  141.5 9.3 %copy-start.3 = (f32[32,4096]{1,0:T(8,128)S(1)}, f32[32,4096]{1,0:T(8,128)}, u32[]{:S(2)}) copy-start(f32[32,4096]{1,0:T(8,128)} %get-tuple-element.17) | copy-start | bytes 1572868
  141.5 10.1 %copy-start.2 = (f32[32,4096]{1,0:T(8,128)S(1)}, f32[32,4096]{1,0:T(8,128)}, u32[]{:S(2)}) copy-start(f32[32,4096]{1,0:T(8,128)} %get-tuple-element.18) | copy-start | bytes 1572868

commit v2 on v1

--- a/solution.py
+++ b/solution.py
@@ -9,7 +9,7 @@
 
 STEP = 4
 CHUNKS = 8
-PIECES = 2
+PIECES = 4
 ROW_TILE = 16
 MESH_ID = pl.DeviceIdType.MESH
 BF16 = jnp.bfloat16
@@ -26,9 +26,9 @@
 def kernel(
     n_dp, n_f,
     tok_hbm, gain_ref, w_hbm, cot_ref, basis_ref, m_ref, v_ref,
-    keys_ref, m_out, v_out, whole_out,
-    normed, w_all, proj, core_tx, core_rx, x_tx, x_rx, y_tx, y_rx, z_own, z_tx, z_rx,
-    whole, acc,
+    keys_ref, m_out, v_out, update_out,
+    normed, w_all, proj, core_tx, core_rx, x_tx, x_rx, y_tx, y_rx, ya_tx, ya_rx, xb_tx, xb_rx,
+    z_own, z_tx, z_rx, whole, acc, u_buf,
     load_sem, core_s, core_r, x_s, x_r, y_s, y_r, z_s, z_r,
     gz_s, gz_r, gx_s, gx_r, gc_s, gc_r, w1_s, w1_r, w2_s, w2_r, w3_s, w3_r, out_sem,
 ):
@@ -92,9 +92,12 @@
         blk = w_all.at[at_y(k), w_rows(pair_q, p)]
         return remote(blk, blk, w3_s.at[p, k - 1], w3_r.at[p, k - 1], dev_core)
 
-    for p in range(PIECES):
+    def w_begin(p):
         for k in range(1, n_f):
             w1(p, k).start()
+
+    w_begin(0)
+    w_begin(1)
 
     load_w = pltpu.make_async_copy(w_hbm, w_all.at[y], load_sem.at[1])
     load_w.start()
@@ -125,11 +128,22 @@
         return remote(core_tx.at[t], core_rx.at[t], core_s.at[t], core_r.at[t], dev_core)
 
     def x_copy(t):
-        return remote(x_tx.at[t], x_rx.at[t], x_s.at[t], x_r.at[t], dev_x)
+        h = lax.div(t, 2)
+        return remote(x_tx.at[h], x_rx.at[h], x_s.at[t], x_r.at[t], dev_x)
 
     def y_copy(t, k):
-        return remote(y_tx.at[t, k - 1], y_rx.at[t, k - 1], y_s.at[t, k - 1],
+        h = lax.div(t, 2)
+        return remote(y_tx.at[h, k - 1], y_rx.at[h, k - 1], y_s.at[t, k - 1],
                       y_r.at[t, k - 1], (dp, at_y(k)))
+
+    def ya_copy(t, k):
+        h = lax.div(t, 2)
+        return remote(ya_tx.at[h, k - 1], ya_rx.at[h, k - 1], y_s.at[t, k - 1],
+                      y_r.at[t, k - 1], (dp, at_y(k)))
+
+    def xb_copy(t):
+        h = lax.div(t, 2)
+        return remote(xb_tx.at[h], xb_rx.at[h], x_s.at[t], x_r.at[t], dev_x)
 
     def z_copy(t, k):
         return remote(z_tx.at[t, at_z(k)], z_rx.at[t, k - 1], z_s.at[t, k - 1],
@@ -153,34 +167,64 @@
             core_tx[t, f] = part(lhs, f, t).astype(BF16).reshape(core_tx.shape[2:])
         core_copy(t).start()
 
-    def stage_x(t):
+    def core_sum(f, t, xi):
+        mine = part(proj[:, xi, core].reshape(n_z * r, rows), f, t).reshape(n_z, r, cw)
+        return mine + core_rx[t, f, :, xi].astype(F32)
+
+    def even_first(t):
         core_copy(t).wait_recv()
-        lhs = proj[:, other_x, core].reshape(n_z * r, rows)
         for f in range(n_f):
-            mine = part(lhs, f, t).reshape(n_z, r, cw)
-            x_tx[t, f] = (mine + core_rx[t, f, :, other_x].astype(F32)).astype(BF16)
+            x_tx[lax.div(t, 2), f] = core_sum(f, t, other_x).astype(BF16)
         x_copy(t).start()
 
-    def chip_sum(f, t):
-        mine = part(proj[:, x, core].reshape(n_z * r, rows), f, t).reshape(n_z, r, cw)
-        return mine + core_rx[t, f, :, x].astype(F32) + x_rx[t, f].astype(F32)
-
-    def stage_y(t):
+    def even_second(t):
+        h = lax.div(t, 2)
         x_copy(t).wait_recv()
         for k in range(1, n_f):
-            y_tx[t, k - 1] = chip_sum(at_y(k), t).astype(BF16)
+            f = at_y(k)
+            y_tx[h, k - 1] = (core_sum(f, t, x) + x_rx[h, f].astype(F32)).astype(BF16)
             y_copy(t, k).start()
 
-    def stage_z(t):
-        for k in range(1, n_f):
-            y_copy(t, k).wait_recv()
-        total = chip_sum(y, t)
-        for k in range(1, n_f):
-            total = total + y_rx[t, k - 1].astype(F32)
+    def send_z(t, total):
         z_own[t] = total
         z_tx[t] = total.astype(BF16)
         for k in range(1, n_z):
             z_copy(t, k).start()
+
+    def even_third(t):
+        h = lax.div(t, 2)
+        for k in range(1, n_f):
+            y_copy(t, k).wait_recv()
+        total = core_sum(y, t, x) + x_rx[h, y].astype(F32)
+        for k in range(1, n_f):
+            total = total + y_rx[h, k - 1].astype(F32)
+        send_z(t, total)
+
+    def odd_first(t):
+        h = lax.div(t, 2)
+        core_copy(t).wait_recv()
+        lhs = proj[:, :, core].reshape(n_z * 2 * r, rows)
+        for k in range(1, n_f):
+            f = at_y(k)
+            mine = part(lhs, f, t).reshape(n_z, 2, r, cw)
+            ya_tx[h, k - 1] = (mine + core_rx[t, f].astype(F32)).astype(BF16)
+            ya_copy(t, k).start()
+
+    def odd_sum(t, xi):
+        total = core_sum(y, t, xi)
+        for k in range(1, n_f):
+            total = total + ya_rx[lax.div(t, 2), k - 1, :, xi].astype(F32)
+        return total
+
+    def odd_second(t):
+        for k in range(1, n_f):
+            ya_copy(t, k).wait_recv()
+        xb_tx[lax.div(t, 2)] = odd_sum(t, other_x).astype(BF16)
+        xb_copy(t).start()
+
+    def odd_third(t):
+        xb_copy(t).wait_recv()
+        send_z(t, odd_sum(t, x) + xb_rx[lax.div(t, 2)].astype(F32))
 
     def stage_adam(t):
         for k in range(1, n_z):
@@ -208,9 +252,39 @@
         gx_send(t).wait_recv()
         gc_send(t).start()
 
-    def keys_part(f, t):
-        rhs = w_all[f, pl.ds(pl.multiple_of(t * cw, cw), cw), :]
-        return jnp.dot(normed[:, cols(f, t)], rhs, preferred_element_type=F32)
+    def update_copy(t):
+        return pltpu.make_async_copy(
+            u_buf.at[lax.rem(t, 2)],
+            update_out.at[pl.ds(pl.multiple_of(t * cw, cw), cw), :],
+            out_sem.at[lax.rem(t, 2)],
+        )
+
+    def stage_update(t):
+        gc_send(t).wait_recv()
+
+        @pl.when(t >= 2)
+        def _():
+            update_copy(t - 2).wait()
+
+        back = lax.dot_general(
+            whole[t].reshape(n_z * 4 * r, cw), basis_ref[...], (((0,), (1,)), ((), ())),
+            preferred_element_type=F32,
+        )
+        u_buf[lax.rem(t, 2)] = (0.25 * back).astype(BF16)
+        update_copy(t).start()
+
+    kv = acc.shape[1]
+    n_tile = 256
+    n_cols = kv // n_tile
+
+    def keys_part(f, n):
+        sl = pl.ds(pl.multiple_of(n * n_tile, n_tile), n_tile)
+        lhs = normed[:, pl.ds(pl.multiple_of(f * d_f, d_f), d_f)]
+        return sl, jnp.dot(lhs, w_all[f, :, sl], preferred_element_type=F32)
+
+    def stage_keys(n):
+        sl, own = keys_part(y, n)
+        acc[:, sl] = own
 
     def w_forward(p):
         for k in range(1, n_f):
@@ -224,26 +298,39 @@
             w3(p, k).start()
 
     load_w.wait()
-    acc[...] = jnp.zeros_like(acc)
-    stages = [stage_core, stage_x, stage_y, stage_z, stage_adam, stage_gx, stage_gc]
-    w_steps = {4: [(w_forward, 0)], 6: [(w_forward, 1)], 9: [(w_last, 0)], 12: [(w_last, 1)]}
-
-    @pl.loop(0, CHUNKS + len(stages) - 1)
+    stages = [
+        (0, stage_core, stage_core), (1, even_first, odd_first), (3, even_second, odd_second),
+        (5, even_third, odd_third), (7, stage_adam, stage_adam), (9, stage_gx, stage_gx),
+        (11, stage_gc, stage_gc), (13, stage_update, stage_update),
+    ]
+    w_steps = {
+        5: (w_forward, 0), 7: (w_forward, 1), 12: (w_forward, 2), 14: (w_forward, 3),
+        8: (w_last, 0), 10: (w_last, 1), 15: (w_last, 2), 17: (w_last, 3),
+    }
+    w_starts = {8: 2, 10: 3}
+
+    def run_if(cond, stage, t):
+        @pl.when(cond)
+        def _():
+            stage(t)
+
+    @pl.loop(0, CHUNKS + 13)
     def _(s):
-        for lag, stage in reversed(list(enumerate(stages))):
-            @pl.when(jnp.logical_and(s >= lag, s < CHUNKS + lag))
-            def _():
-                stage(s - lag)
-
-        @pl.when(s < CHUNKS)
-        def _():
-            acc[...] += keys_part(y, s)
-
-        for at, calls in w_steps.items():
-            @pl.when(s == at)
-            def _():
-                for call, p in calls:
-                    call(p)
+        for at, p in w_starts.items():
+            run_if(s == at, w_begin, p)
+        for lag, even, odd in stages:
+            t = s - lag
+            live = jnp.logical_and(t >= 0, t < CHUNKS)
+            if even is odd:
+                run_if(live, even, t)
+            else:
+                run_if(jnp.logical_and(live, lax.rem(s, 2) == lag % 2), even, t)
+                run_if(jnp.logical_and(live, lax.rem(s, 2) != lag % 2), odd, t)
+            if lag == 1:
+                run_if(jnp.logical_and(s >= CHUNKS + 1, s < CHUNKS + 1 + n_cols),
+                       stage_keys, s - CHUNKS - 1)
+        for at, (call, p) in w_steps.items():
+            run_if(s == at, call, p)
 
     for p in range(PIECES):
         for k in range(1, n_f):
@@ -251,32 +338,28 @@
             w3(p, k).wait_recv()
 
     for k in range(1, n_f):
-        @pl.loop(0, CHUNKS)
-        def _(t):
-            acc[...] += keys_part(at_y(k), t)
+        @pl.loop(0, n_cols)
+        def _(n):
+            sl, term = keys_part(at_y(k), n)
+            acc[:, sl] += term
 
     keys_ref[...] = acc[...].astype(BF16)
-
-    def out_copy(t):
-        return pltpu.make_async_copy(whole.at[t], whole_out.at[t], out_sem.at[t])
-
-    @pl.loop(0, CHUNKS)
-    def _(t):
-        gc_send(t).wait_recv()
-        out_copy(t).start()
+    update_copy(CHUNKS - 2).wait()
+    update_copy(CHUNKS - 1).wait()
 
     @pl.loop(0, CHUNKS)
     def _(t):
         core_copy(t).wait_send()
-        x_copy(t).wait_send()
-        for k in range(1, n_f):
-            y_copy(t, k).wait_send()
+        run_if(lax.rem(t, 2) == 0, lambda u: x_copy(u).wait_send(), t)
+        run_if(lax.rem(t, 2) == 1, lambda u: xb_copy(u).wait_send(), t)
+        for k in range(1, n_f):
+            run_if(lax.rem(t, 2) == 0, lambda u: y_copy(u, k).wait_send(), t)
+            run_if(lax.rem(t, 2) == 1, lambda u: ya_copy(u, k).wait_send(), t)
         for k in range(1, n_z):
             z_copy(t, k).wait_send()
             gz_send(t, k).wait_send()
         gx_send(t).wait_send()
         gc_send(t).wait_send()
-        out_copy(t).wait()
 
     for p in range(PIECES):
         for k in range(1, n_f):
@@ -297,13 +380,13 @@
     vm = pl.BlockSpec(memory_space=pltpu.VMEM)
     hbm = pl.BlockSpec(memory_space=pl.ANY)
     dma = pltpu.SemaphoreType.DMA
-    keys, m_new, v_new, whole = pl.pallas_call(
+    return pl.pallas_call(
         functools.partial(kernel, n_dp, n_f),
         out_shape=(
             jax.ShapeDtypeStruct((rows, kv), BF16),
             jax.ShapeDtypeStruct(exp_avg.shape, F32),
             jax.ShapeDtypeStruct(exp_avg.shape, F32),
-            jax.ShapeDtypeStruct((c, n_z, 2, 2, r, cw), BF16),
+            jax.ShapeDtypeStruct((d_f, kv), BF16),
         ),
         in_specs=[hbm, vm, hbm, vm, vm, vm, vm],
         out_specs=(vm, vm, vm, hbm),
@@ -313,15 +396,20 @@
             pltpu.VMEM((n_z, 2, 2, r, rows), BF16),
             pltpu.VMEM((c, n_f, n_z, 2, r, cw), BF16),
             pltpu.VMEM((c, n_f, n_z, 2, r, cw), BF16),
-            pltpu.VMEM((c, n_f, n_z, r, cw), BF16),
-            pltpu.VMEM((c, n_f, n_z, r, cw), BF16),
-            pltpu.VMEM((c, n_f - 1, n_z, r, cw), BF16),
-            pltpu.VMEM((c, n_f - 1, n_z, r, cw), BF16),
+            pltpu.VMEM((c // 2, n_f, n_z, r, cw), BF16),
+            pltpu.VMEM((c // 2, n_f, n_z, r, cw), BF16),
+            pltpu.VMEM((c // 2, n_f - 1, n_z, r, cw), BF16),
+            pltpu.VMEM((c // 2, n_f - 1, n_z, r, cw), BF16),
+            pltpu.VMEM((c // 2, n_f - 1, n_z, 2, r, cw), BF16),
+            pltpu.VMEM((c // 2, n_f - 1, n_z, 2, r, cw), BF16),
+            pltpu.VMEM((c // 2, n_z, r, cw), BF16),
+            pltpu.VMEM((c // 2, n_z, r, cw), BF16),
             pltpu.VMEM((c, n_z, r, cw), F32),
             pltpu.VMEM((c, n_z, r, cw), BF16),
             pltpu.VMEM((c, n_z - 1, r, cw), BF16),
             pltpu.VMEM((c, n_z, 2, 2, r, cw), BF16),
             pltpu.VMEM((rows, kv), F32),
+            pltpu.VMEM((2, cw, kv), BF16),
             dma((2,)),
             dma((c,)), dma((c,)),
             dma((c,)), dma((c,)),
@@ -333,17 +421,12 @@
             dma((PIECES, n_f - 1)), dma((PIECES, n_f - 1)),
             dma((PIECES, n_f - 1, 2)), dma((PIECES, n_f - 1, 2)),
             dma((PIECES, n_f - 1)), dma((PIECES, n_f - 1)),
-            dma((c,)),
+            dma((2,)),
         ],
         compiler_params=pltpu.CompilerParams(
             collective_id=0, has_side_effects=True, vmem_limit_bytes=60 * 2**20
         ),
     )(tokens, norm_gain.reshape(1, d), key_weight, key_cotangent, basis, exp_avg, exp_avg_sq)
-    back = lax.dot_general(
-        whole.reshape(c, rank, cw), basis, (((1,), (1,)), ((), ())), preferred_element_type=F32
-    )
-    update = (0.25 * back).astype(BF16).reshape(d_f, kv)
-    return keys, m_new, v_new, update
 
 
 def solution(mesh):

time: 153 us -> 125 us (0.82)
  Pallas kernels: 139 us -> 111 us
  local copies, waits for them, and re-layouts: 3.77 us -> 12.9 us
  matrix products: 8.51 us -> 0 us
    pallas_call x1, Pallas kernels: 139 us -> 111 us  [per_device(): pl.pallas_call(functools.partial(kernel, n_dp, n_f), out_shape=(jax.Shape...]
    unnamed x11 -> x4, local copies, waits for them, and re-layouts: 2.42 us -> 11.5 us
    dot_general x1 -> x0, matrix products: 8.51 us -> none  [per_device(): lax.dot_general(whole.reshape(c, rank, cw), basis, (((1,), (1,)), ((), ()...]
where the time goes in v2:
time: 125 us; the launch traced here: 124 us
  Pallas kernels  111 us (89%)
  local copies, waits for them, and re-layouts  12.9 us (10%)
    pallas_call x1, Pallas kernels, per_device(): pl.pallas_call(functools.partial(kernel, n_dp, n_f), out_shape=(jax.Shape...  111 us
    unnamed x4, local copies, waits for them, and re-layouts  11.5 us

profile of v2, /device:TPU:0, one launch (start us, length us, event | category | flops | bytes accessed | tf_op | source)
XLA Modules:
  0.0 124.4 jit_solution(7553298097978272643)
XLA Ops:
  0.6 1.4 %reshape.11.gain_ref = bf16[1,8192]{1,0:T(2,128)(2,1)} reshape(bf16[8192]{0:T(1024)(128)(2,1)} %param.8) | data formatting | bytes 32768 | tf_op jit(solution)/shard_map/reshape | solution.py:429
  2.0 110.9 %shard_map.102 = (bf16[384,768]{1,0:T(8,128)(2,1)}, f32[32,4096]{1,0:T(8,128)}, f32[32,4096]{1,0:T(8,128)}, bf16[4096,768]{1,0:T(8,128)(2,1)}) custom-call(bf16[384,8192]{1,0:T(8,128)(2,1)} %tok_hbm.1, bf16[1,8192]{1,0:T(2,128)(2,1)} %reshape.11.gain_ref, bf16[4096,768]{1,0:T(8,128)(2,1)} %w_hbm.1, bf16[384,768]{1,0:T(8,128)(2,1)} %cot_ref.1, ...), custom_call_target="tpu_custom_call" | custom-call | tf_op jit(solution)/shard_map/pallas_call | solution.py:383
  112.9 1.9 %copy.15 = bf16[384,768]{1,0:T(8,128)(2,1)} copy(bf16[384,768]{1,0:T(8,128)(2,1)} %get-tuple-element.8) | data formatting | bytes 1179648
  114.8 1.9 %copy.16 = f32[32,4096]{1,0:T(8,128)} copy(f32[32,4096]{1,0:T(8,128)} %get-tuple-element.9) | data formatting | bytes 1048576
  116.6 1.9 %copy.17 = f32[32,4096]{1,0:T(8,128)} copy(f32[32,4096]{1,0:T(8,128)} %get-tuple-element.10) | data formatting | bytes 1048576
  118.5 5.9 %copy.18 = bf16[4096,768]{1,0:T(8,128)(2,1)} copy(bf16[4096,768]{1,0:T(8,128)(2,1)} %get-tuple-element.11) | data formatting | bytes 12582912

commit v3 on v2

--- a/solution.py
+++ b/solution.py
@@ -27,8 +27,8 @@
     n_dp, n_f,
     tok_hbm, gain_ref, w_hbm, cot_ref, basis_ref, m_ref, v_ref,
     keys_ref, m_out, v_out, update_out,
-    normed, w_all, proj, core_tx, core_rx, x_tx, x_rx, y_tx, y_rx, ya_tx, ya_rx, xb_tx, xb_rx,
-    z_own, z_tx, z_rx, whole, acc, u_buf,
+    normed, w_all, whole_rank, proj, core_tx, core_rx, x_tx, x_rx, y_tx, y_rx, ya_tx, ya_rx, xb_tx, xb_rx,
+    own, z_tx, z_rx, whole, acc, u_buf,
     load_sem, core_s, core_r, x_s, x_r, y_s, y_r, z_s, z_r,
     gz_s, gz_r, gx_s, gx_r, gc_s, gc_r, w1_s, w1_r, w2_s, w2_r, w3_s, w3_r, out_sem,
 ):
@@ -56,7 +56,7 @@
     d_f = w_hbm.shape[0]
     rows, d = normed.shape
     cw = d_f // CHUNKS
-    r = proj.shape[3]
+    r = whole_rank.shape[3]
     quarter = d_f // 4
     piece = quarter // PIECES
 
@@ -105,11 +105,14 @@
     projected = lax.dot_general(
         basis_ref[...], cot_ref[...], (((0,), (1,)), ((), ())), preferred_element_type=F32
     ).astype(BF16)
-    proj[...] = projected.reshape(proj.shape)
+    whole_rank[...] = projected.reshape(whole_rank.shape)
+    for i, c_i in enumerate((core, other_core)):
+        for j, x_j in enumerate((x, other_x)):
+            proj[i, j] = whole_rank[:, x_j, c_i]
 
     load_tok.wait()
 
-    gain = gain_ref[...].astype(F32)
+    gain = gain_ref[...].astype(F32).reshape(1, d)
 
     @pl.loop(0, rows // ROW_TILE)
     def _(i):
@@ -121,9 +124,6 @@
     def cols(f, t):
         return pl.ds(pl.multiple_of(f * d_f + t * cw, cw), cw)
 
-    def part(lhs, f, t):
-        return jnp.dot(lhs, normed[:, cols(f, t)], preferred_element_type=F32)
-
     def core_copy(t):
         return remote(core_tx.at[t], core_rx.at[t], core_s.at[t], core_r.at[t], dev_core)
 
@@ -162,31 +162,32 @@
         return remote(blk, blk, gc_s.at[t], gc_r.at[t], dev_core)
 
     def stage_core(t):
-        lhs = proj[:, :, other_core].reshape(n_z * 2 * r, rows)
-        for f in range(n_f):
-            core_tx[t, f] = part(lhs, f, t).astype(BF16).reshape(core_tx.shape[2:])
+        lhs = proj[...].reshape(4 * n_z * r, rows)
+        half = 2 * n_z * r
+        for k in range(n_f):
+            term = jnp.dot(lhs, normed[:, cols(at_y(k), t)], preferred_element_type=F32)
+            own[t, k] = term[:half].reshape(2, n_z, r, cw)
+            core_tx[t, k] = term[half:].astype(BF16).reshape(2, n_z, r, cw)
         core_copy(t).start()
 
-    def core_sum(f, t, xi):
-        mine = part(proj[:, xi, core].reshape(n_z * r, rows), f, t).reshape(n_z, r, cw)
-        return mine + core_rx[t, f, :, xi].astype(F32)
+    def core_sum(t, k, xi):
+        return own[t, k, xi] + core_rx[t, k, xi].astype(F32)
 
     def even_first(t):
         core_copy(t).wait_recv()
-        for f in range(n_f):
-            x_tx[lax.div(t, 2), f] = core_sum(f, t, other_x).astype(BF16)
+        for k in range(n_f):
+            x_tx[lax.div(t, 2), k] = core_sum(t, k, 1).astype(BF16)
         x_copy(t).start()
 
     def even_second(t):
         h = lax.div(t, 2)
         x_copy(t).wait_recv()
         for k in range(1, n_f):
-            f = at_y(k)
-            y_tx[h, k - 1] = (core_sum(f, t, x) + x_rx[h, f].astype(F32)).astype(BF16)
+            y_tx[h, k - 1] = (core_sum(t, k, 0) + x_rx[h, k].astype(F32)).astype(BF16)
             y_copy(t, k).start()
 
     def send_z(t, total):
-        z_own[t] = total
+        own[t, 0, 0] = total
         z_tx[t] = total.astype(BF16)
         for k in range(1, n_z):
             z_copy(t, k).start()
@@ -195,7 +196,7 @@
         h = lax.div(t, 2)
         for k in range(1, n_f):
             y_copy(t, k).wait_recv()
-        total = core_sum(y, t, x) + x_rx[h, y].astype(F32)
+        total = core_sum(t, 0, 0) + x_rx[h, 0].astype(F32)
         for k in range(1, n_f):
             total = total + y_rx[h, k - 1].astype(F32)
         send_z(t, total)
@@ -203,33 +204,31 @@
     def odd_first(t):
         h = lax.div(t, 2)
         core_copy(t).wait_recv()
-        lhs = proj[:, :, core].reshape(n_z * 2 * r, rows)
-        for k in range(1, n_f):
-            f = at_y(k)
-            mine = part(lhs, f, t).reshape(n_z, 2, r, cw)
-            ya_tx[h, k - 1] = (mine + core_rx[t, f].astype(F32)).astype(BF16)
+        for k in range(1, n_f):
+            for xi in range(2):
+                ya_tx[h, k - 1, xi] = core_sum(t, k, xi).astype(BF16)
             ya_copy(t, k).start()
 
     def odd_sum(t, xi):
-        total = core_sum(y, t, xi)
-        for k in range(1, n_f):
-            total = total + ya_rx[lax.div(t, 2), k - 1, :, xi].astype(F32)
+        total = core_sum(t, 0, xi)
+        for k in range(1, n_f):
+            total = total + ya_rx[lax.div(t, 2), k - 1, xi].astype(F32)
         return total
 
     def odd_second(t):
         for k in range(1, n_f):
             ya_copy(t, k).wait_recv()
-        xb_tx[lax.div(t, 2)] = odd_sum(t, other_x).astype(BF16)
+        xb_tx[lax.div(t, 2)] = odd_sum(t, 1).astype(BF16)
         xb_copy(t).start()
 
     def odd_third(t):
         xb_copy(t).wait_recv()
-        send_z(t, odd_sum(t, x) + xb_rx[lax.div(t, 2)].astype(F32))
+        send_z(t, odd_sum(t, 0) + xb_rx[lax.div(t, 2)].astype(F32))
 
     def stage_adam(t):
         for k in range(1, n_z):
             z_copy(t, k).wait_recv()
-        grad = z_own[t, z]
+        grad = own[t, 0, 0, z]
         for k in range(1, n_z):
             grad = grad + z_rx[t, k - 1].astype(F32)
         sl = pl.ds(pl.multiple_of(t * cw, cw), cw)
@@ -394,17 +393,18 @@
             pltpu.VMEM((rows, d), BF16),
             pltpu.VMEM((n_f, d_f, kv), BF16),
             pltpu.VMEM((n_z, 2, 2, r, rows), BF16),
-            pltpu.VMEM((c, n_f, n_z, 2, r, cw), BF16),
-            pltpu.VMEM((c, n_f, n_z, 2, r, cw), BF16),
+            pltpu.VMEM((2, 2, n_z, r, rows), BF16),
+            pltpu.VMEM((c, n_f, 2, n_z, r, cw), BF16),
+            pltpu.VMEM((c, n_f, 2, n_z, r, cw), BF16),
             pltpu.VMEM((c // 2, n_f, n_z, r, cw), BF16),
             pltpu.VMEM((c // 2, n_f, n_z, r, cw), BF16),
             pltpu.VMEM((c // 2, n_f - 1, n_z, r, cw), BF16),
             pltpu.VMEM((c // 2, n_f - 1, n_z, r, cw), BF16),
-            pltpu.VMEM((c // 2, n_f - 1, n_z, 2, r, cw), BF16),
-            pltpu.VMEM((c // 2, n_f - 1, n_z, 2, r, cw), BF16),
+            pltpu.VMEM((c // 2, n_f - 1, 2, n_z, r, cw), BF16),
+            pltpu.VMEM((c // 2, n_f - 1, 2, n_z, r, cw), BF16),
             pltpu.VMEM((c // 2, n_z, r, cw), BF16),
             pltpu.VMEM((c // 2, n_z, r, cw), BF16),
-            pltpu.VMEM((c, n_z, r, cw), F32),
+            pltpu.VMEM((c, n_f, 2, n_z, r, cw), F32),
             pltpu.VMEM((c, n_z, r, cw), BF16),
             pltpu.VMEM((c, n_z - 1, r, cw), BF16),
             pltpu.VMEM((c, n_z, 2, 2, r, cw), BF16),
@@ -426,7 +426,7 @@
         compiler_params=pltpu.CompilerParams(
             collective_id=0, has_side_effects=True, vmem_limit_bytes=60 * 2**20
         ),
-    )(tokens, norm_gain.reshape(1, d), key_weight, key_cotangent, basis, exp_avg, exp_avg_sq)
+    )(tokens, norm_gain, key_weight, key_cotangent, basis, exp_avg, exp_avg_sq)
 
 
 def solution(mesh):

time: 125 us -> 123 us (0.984)
  local copies, waits for them, and re-layouts: 12.9 us -> 11.5 us
    reshape x1 -> x0, local copies, waits for them, and re-layouts: 1.35 us -> none  [per_device(): norm_gain.reshape(1, d)]
where the time goes in v3:
time: 123 us
  Pallas kernels  111 us (90%)
  local copies, waits for them, and re-layouts  11.5 us (9%)
    pallas_call x1, Pallas kernels, per_device(): pl.pallas_call(functools.partial(kernel, n_dp, n_f), out_shape=(jax.Shape...  111 us
    unnamed x4, local copies, waits for them, and re-layouts  11.5 us

profile of v3, /device:TPU:0, one launch (start us, length us, event | category | flops | bytes accessed | tf_op | source)
XLA Modules:
  0.0 122.9 jit_solution(18041815253527907752)
XLA Ops:
  0.6 110.7 %shard_map.102 = (bf16[384,768]{1,0:T(8,128)(2,1)}, f32[32,4096]{1,0:T(8,128)}, f32[32,4096]{1,0:T(8,128)}, bf16[4096,768]{1,0:T(8,128)(2,1)}) custom-call(bf16[384,8192]{1,0:T(8,128)(2,1)} %tok_hbm.1, bf16[8192]{0:T(1024)(128)(2,1)} %gain_ref.1, bf16[4096,768]{1,0:T(8,128)(2,1)} %w_hbm.1, bf16[384,768]{1,0:T(8,128)(2,1)} %cot_ref.1, ...), custom_call_target="tpu_custom_call" | custom-call | tf_op jit(solution)/shard_map/pallas_call | solution.py:382
  111.4 1.9 %copy.15 = bf16[384,768]{1,0:T(8,128)(2,1)} copy(bf16[384,768]{1,0:T(8,128)(2,1)} %get-tuple-element.8) | data formatting | bytes 1179648
  113.3 1.9 %copy.16 = f32[32,4096]{1,0:T(8,128)} copy(f32[32,4096]{1,0:T(8,128)} %get-tuple-element.9) | data formatting | bytes 1048576
  115.1 1.9 %copy.17 = f32[32,4096]{1,0:T(8,128)} copy(f32[32,4096]{1,0:T(8,128)} %get-tuple-element.10) | data formatting | bytes 1048576
  117.0 5.9 %copy.18 = bf16[4096,768]{1,0:T(8,128)(2,1)} copy(bf16[4096,768]{1,0:T(8,128)(2,1)} %get-tuple-element.11) | data formatting | bytes 12582912
